TPU v7x, 32 devices: a whole 2x2x4 slice. The times are simulated.
32 devices in a mesh: dom: 4 (over y, x), gx: 4 (over z), gy: 2 (over core).
Axes of the slice: x: 2, y: 2, z: 4, core: 2. Of those that a mesh axis runs over, the one named last changes fastest.
Arguments:
- ensemble: float32 [4, 4, 32, 32, 256], P('dom', None, None, 'gx', 'gy'), may hold values from -6 to 6
- ancestors: int32 [4, 4, 32], P(None, 'gx', 'gy'), may hold values from 0 to 3
- particle_air_drag: float32 [4, 2, 32, 256], P('dom', None, 'gx', 'gy'), may hold values from -6 to 6
- eddy_diffusivity: float32 [31], replicated, may hold values from 0.02 to 0.15
Outputs:
- forecast: float32 [4, 4, 32, 32, 256], P('dom', None, None, 'gx', 'gy')
All inputs are finite; a program needn't handle non-finite values.
Results may differ from a plain program's by a relative error of at most 0.0003.
Values sent between devices are 32-bit elements; how exact they have to be, the bound alone decides.
A program may use at most 64 MiB of HBM per device.

v0:
```python
import functools
import math

import jax
import jax.numpy as jnp
from jax import lax
from jax.experimental import pallas as pl
from jax.experimental.pallas import tpu as pltpu
from jax.sharding import PartitionSpec as P

STEPS = 4
TILE = 8
CHUNK = 8
AHEAD = 2

ADVECT = 0.2
DIFFUSE = 0.15
BUOY_TEMP = 0.2
BUOY_SALT = 0.1
PRESS_SCALE = 0.25
WIND_SCALE = 0.2
CORIO_BASE = 0.1
CORIO_SLOPE = 0.1

MESH = pl.DeviceIdType.MESH
FIELDS = 4
PAIR = 2


def remote(src, dst, send, recv, where):
    return pltpu.make_async_remote_copy(
        src_ref=src,
        dst_ref=dst,
        send_sem=send,
        recv_sem=recv,
        device_id=where,
        device_id_type=MESH,
    )


def kernel(
    slow, fast, n_gx, n_gy, ens_hbm, anc_hbm, drag_hbm, eddy_hbm, out_hbm,
    ens, anc, drag, eddy, out, state_0, state_1, state_2, state_3, sums, ag_f, ag_s, tx_f, tx_s, rx_f, rx_s, hy_out, hy_in,
    local_sem, out_sem, agf_send, agf_recv, ags_send, ags_recv, txf_send, txf_recv, txs_send, txs_recv,
    hx_send, hx_recv, hy_send, hy_recv, drag_send, drag_recv,
):
    levels, rows, cols = ens.shape[2:]
    chunks = levels // CHUNK
    states = (state_0, state_1, state_2, state_3)
    me = lax.axis_index("dom")
    a, b = me // fast, me % fast
    gx, gy = lax.axis_index("gx"), lax.axis_index("gy")
    gx_next, gx_prev = lax.rem(gx + 1, n_gx), lax.rem(gx + n_gx - 1, n_gx)
    has_left, has_right = gy > 0, gy < n_gy - 1

    loads = [
        pltpu.make_async_copy(there, here, local_sem.at[number])
        for number, (there, here) in enumerate(
            ((anc_hbm, anc), (ens_hbm, ens), (eddy_hbm, eddy), (drag_hbm.at[0], drag.at[0]))
        )
    ]
    for load in loads:
        load.start()

    fast_peers = [a * fast + lax.rem(b + j, fast) for j in range(1, fast)]
    slow_peers = [lax.rem(a + i, slow) * fast + b for i in range(1, slow)]

    def fast_peer(j):
        return fast_peers[j - 1]

    def slow_peer(i):
        return slow_peers[i - 1]

    def at_dom(member):
        return (member, gx, gy)

    at_prev, at_next = (me, gx_prev, gy), (me, gx_next, gy)
    at_left, at_right = (me, gx, gy - 1), (me, gx, gy + 1)

    barrier = pltpu.get_barrier_semaphore()
    for j in range(1, fast):
        pl.semaphore_signal(barrier, inc=1, device_id=at_dom(fast_peer(j)), device_id_type=MESH)
    for i in range(1, slow):
        pl.semaphore_signal(barrier, inc=1, device_id=at_dom(slow_peer(i)), device_id_type=MESH)
    for there in (at_next, at_prev):
        pl.semaphore_signal(barrier, inc=1, device_id=there, device_id_type=MESH)

    @pl.when(has_left)
    def _():
        pl.semaphore_signal(barrier, inc=1, device_id=at_left, device_id_type=MESH)

    @pl.when(has_right)
    def _():
        pl.semaphore_signal(barrier, inc=1, device_id=at_right, device_id_type=MESH)

    around = has_left.astype(jnp.int32) + has_right.astype(jnp.int32)
    pl.semaphore_wait(barrier, fast - 1 + slow - 1 + 2 + around)

    def part(c):
        return pl.ds(c * CHUNK, CHUNK)

    def gather_f(j, c):
        return remote(ens.at[0, 0:PAIR, part(c)], ag_f.at[j - 1, :, part(c)],
                      agf_send.at[j - 1, c], agf_recv.at[j - 1, c], at_dom(fast_peer(j)))

    def gather_s(i, c):
        return remote(ens.at[0, PAIR:FIELDS, part(c)], ag_s.at[i - 1, :, part(c)],
                      ags_send.at[i - 1, c], ags_recv.at[i - 1, c], at_dom(slow_peer(i)))

    def onward_f(i, c):
        return remote(tx_f.at[i - 1, :, part(c)], rx_f.at[i - 1, :, part(c)],
                      txf_send.at[i - 1, c], txf_recv.at[i - 1, c], at_dom(slow_peer(i)))

    def onward_s(j, c):
        return remote(tx_s.at[j - 1, :, part(c)], rx_s.at[j - 1, :, part(c)],
                      txs_send.at[j - 1, c], txs_recv.at[j - 1, c], at_dom(fast_peer(j)))

    def row_halo(side, c):
        there = at_prev if side == 0 else at_next
        edge = slice(0, STEPS) if side == 0 else slice(rows - STEPS, rows)
        return remote(state_0.at[0, :, part(c), edge], state_0.at[1, :, part(c), edge],
                      hx_send.at[side, c], hx_recv.at[side, c], there)

    def drag_halo(side):
        there = at_prev if side == 0 else at_next
        edge = slice(0, STEPS) if side == 0 else slice(rows - STEPS, rows)
        return remote(drag.at[0, :, edge], drag.at[1, :, edge],
                      drag_send.at[side], drag_recv.at[side], there)

    def col_halo(step, side, c):
        there = at_right if side == 0 else at_left
        return remote(hy_out.at[step, c], hy_in.at[step, side, c],
                      hy_send.at[step, side, c], hy_recv.at[step, side, c], there)

    def write_out(c):
        return pltpu.make_async_copy(out.at[:, :, part(c)], out_hbm.at[:, :, part(c)], out_sem.at[c])

    def start_columns(step, c):
        @pl.when(has_right)
        def _():
            col_halo(step, 0, c).start()

        @pl.when(has_left)
        def _():
            col_halo(step, 1, c).start()

    def wait_columns(step, c):
        @pl.when(has_left)
        def _():
            col_halo(step, 0, c).wait_recv()

        @pl.when(has_right)
        def _():
            col_halo(step, 1, c).wait_recv()

    def start_gather(c):
        for j in range(1, fast):
            gather_f(j, c).start()
        for i in range(1, slow):
            gather_s(i, c).start()

    loads[1].wait()
    for c in range(min(AHEAD, chunks)):
        start_gather(c)

    @pl.when(jnp.logical_not(has_left))
    def _():
        hy_in[:, 0] = jnp.zeros((STEPS, chunks, rows, cols), jnp.float32)

    @pl.when(jnp.logical_not(has_right))
    def _():
        hy_in[:, 1] = jnp.zeros((STEPS, chunks, rows, cols), jnp.float32)

    sums[...] = jnp.zeros(sums.shape, jnp.float32)
    row = lax.broadcasted_iota(jnp.int32, (rows, cols), 0)
    lane = lax.broadcasted_iota(jnp.int32, (rows, cols), 1)
    loads[0].wait()

    def sources_of(member):
        total = jnp.zeros((rows, cols), jnp.int32)
        for tx in range(rows // TILE):
            for ty in range(cols // TILE):
                here = (lane >= ty * TILE) & (lane < (ty + 1) * TILE)
                if rows > TILE:
                    here = here & (row >= tx * TILE) & (row < (tx + 1) * TILE)
                total = jnp.where(here, anc[member, tx, ty], total)
        return total

    wanted_f = [sources_of(slow_peer(i)) for i in range(1, slow)]
    wanted_s = [sources_of(fast_peer(j)) for j in range(1, fast)]
    mine = sources_of(me)
    held_f = [a * fast + lax.rem(b + fast - j, fast) for j in range(1, fast)]
    held_s = [lax.rem(a + slow - i, slow) * fast + b for i in range(1, slow)]
    from_f = []
    for i in range(1, slow):
        base = lax.rem(a + slow - i, slow) * fast
        from_f.append((mine >= base) & (mine < base + fast))
    from_s = []
    for j in range(1, fast):
        base = lax.rem(b + fast - j, fast)
        hit = mine == base
        for i in range(1, slow):
            hit = hit | (mine == base + i * fast)
        from_s.append(hit)
    for load in loads[2:]:
        load.wait()
    drag_halo(0).start()
    drag_halo(1).start()

    def pass_on(c):
        for j in range(1, fast):
            gather_f(j, c).wait_recv()
        for i in range(1, slow):
            for f in range(PAIR):
                for kk in range(CHUNK):
                    k = c * CHUNK + kk
                    value = ens[0, f, k]
                    for j in range(1, fast):
                        value = jnp.where(wanted_f[i - 1] == held_f[j - 1], ag_f[j - 1, f, k], value)
                    tx_f[i - 1, f, k] = value
            onward_f(i, c).start()
        for i in range(1, slow):
            gather_s(i, c).wait_recv()
        for j in range(1, fast):
            for f in range(PAIR):
                for kk in range(CHUNK):
                    k = c * CHUNK + kk
                    value = ens[0, PAIR + f, k]
                    for i in range(1, slow):
                        value = jnp.where(wanted_s[j - 1] == held_s[i - 1], ag_s[i - 1, f, k], value)
                    tx_s[j - 1, f, k] = value
            onward_s(j, c).start()

        @pl.when(c + AHEAD < chunks)
        def _():
            start_gather(c + AHEAD)

    blank = jnp.zeros((rows, cols), jnp.float32)

    def place_of(tile, f, kk):
        return 2 * ((tile * FIELDS + f) * CHUNK + kk)

    couple = lane >> 1

    def pack(q, place, packed):
        turned = pltpu.roll(q, (place + 1) % cols, 1)
        return jnp.where(couple == place // 2, turned, packed)

    def resample(c):
        for i in range(1, slow):
            onward_f(i, c).wait_recv()
        for j in range(1, fast):
            onward_s(j, c).wait_recv()
        for kk in range(CHUNK):
            k = c * CHUNK + kk
            for f in range(FIELDS):
                q = ens[0, f, k]
                if f < PAIR:
                    for j in range(1, fast):
                        q = jnp.where(mine == held_f[j - 1], ag_f[j - 1, f, k], q)
                    for i in range(1, slow):
                        q = jnp.where(from_f[i - 1], rx_f[i - 1, f, k], q)
                else:
                    for i in range(1, slow):
                        q = jnp.where(mine == held_s[i - 1], ag_s[i - 1, f - PAIR, k], q)
                    for j in range(1, fast):
                        q = jnp.where(from_s[j - 1], rx_s[j - 1, f - PAIR, k], q)
                state_0[0, f, k] = q
        row_halo(0, c).start()
        row_halo(1, c).start()

    def first_columns(c):
        row_halo(0, c).wait_recv()
        row_halo(1, c).wait_recv()
        packed = blank
        for tile in range(2):
            for f in range(FIELDS):
                for kk in range(CHUNK):
                    packed = pack(state_0[tile, f, c * CHUNK + kk], place_of(tile, f, kk), packed)
        hy_out[0, c] = packed
        start_columns(0, c)

    positions = (gy * cols + lane).astype(jnp.float32)
    coriolis = CORIO_BASE + CORIO_SLOPE * (positions + 0.5) / (n_gy * cols)
    half = 0.5 * ADVECT
    temp, salt = 0.5 * PRESS_SCALE * BUOY_TEMP, 0.5 * PRESS_SCALE * BUOY_SALT

    def advance(step, c):
        final = step == STEPS - 1
        now_ref, later_ref = states[step], None if final else states[step + 1]
        tiles = (0,) if final else (0, 1)
        wait_columns(step, c)
        columns = jnp.where(lane % 2 == 0, hy_in[step, 0, c], hy_in[step, 1, c])
        packed = blank
        press_x = [sums[step, t, 0] for t in tiles]
        press_y = [sums[step, t, 1] for t in tiles]
        flux = [[sums[step, t, 2 + f] for f in range(FIELDS)] for t in tiles]
        for kk in range(CHUNK):
            k = c * CHUNK + kk
            below = jnp.minimum(k + 1, levels - 1)
            mixing = eddy[jnp.minimum(k, levels - 2)]
            now = [[now_ref[t, f, k] for f in range(FIELDS)] for t in (0, 1)]
            result = [[None] * FIELDS for t in tiles]
            coef = []
            for t in tiles:
                u, v = now[t][0], now[t][1]
                coef.append((DIFFUSE + half * u, DIFFUSE - half * u, DIFFUSE + half * v, DIFFUSE - half * v))
            diff_x, diff_y = [[] for t in tiles], [[] for t in tiles]
            for f in range(FIELDS):
                up = [pltpu.roll(now[t][f], 1, 0) for t in (0, 1)]
                down = [pltpu.roll(now[t][f], rows - 1, 0) for t in (0, 1)]
                for t in tiles:
                    q = now[t][f]
                    x_m = jnp.where(row == 0, up[1 - t], up[t])
                    x_p = jnp.where(row == rows - 1, down[1 - t], down[t])
                    edge = pltpu.roll(columns, cols - 1 - place_of(t, f, kk), 1)
                    y_m = pltpu.roll(jnp.where(lane == cols - 1, edge, q), 1, 1)
                    y_p = pltpu.roll(jnp.where(lane == 0, edge, q), cols - 1, 1)
                    flow = mixing * (now_ref[t, f, below] - q)
                    total = (1.0 - 4.0 * DIFFUSE) * q + (flow - flux[t][f])
                    c_xm, c_xp, c_ym, c_yp = coef[t]
                    total = total + (c_xp * x_p + c_xm * x_m) + (c_yp * y_p + c_ym * y_m)
                    result[t][f] = total
                    flux[t][f] = flow
                    if f >= PAIR:
                        diff_x[t].append(x_p - x_m)
                        diff_y[t].append(y_p - y_m)
            for t in tiles:
                press_x[t] = press_x[t] + (temp * diff_x[t][0] - salt * diff_x[t][1])
                press_y[t] = press_y[t] + (temp * diff_y[t][0] - salt * diff_y[t][1])
                result[t][0] = result[t][0] + (coriolis * now[t][1] - press_x[t])
                result[t][1] = result[t][1] - (coriolis * now[t][0] + press_y[t])
                if kk == 0:
                    top = jnp.where(c == 0, WIND_SCALE, 0.0)
                    result[t][0] = result[t][0] + top * drag[t, 0]
                    result[t][1] = result[t][1] + top * drag[t, 1]
                for f in range(FIELDS):
                    if final:
                        out[0, f, k] = result[t][f]
                    else:
                        later_ref[t, f, k] = result[t][f]
                        packed = pack(result[t][f], place_of(t, f, kk), packed)
        for t in tiles:
            sums[step, t, 0] = press_x[t]
            sums[step, t, 1] = press_y[t]
            for f in range(FIELDS):
                sums[step, t, 2 + f] = flux[t][f]
        if final:
            write_out(c).start()
        else:
            hy_out[step + 1, c] = packed
            start_columns(step + 1, c)

    drag_halo(0).wait_recv()
    drag_halo(1).wait_recv()

    def tick(t, _):
        def at(c, body):
            @pl.when((c >= 0) & (c < chunks))
            def _():
                body(c)

        at(t, pass_on)
        at(t - 1, resample)
        at(t - 2, first_columns)

        for step in range(STEPS):
            at(t - 3 - step, functools.partial(advance, step))
        return 0

    lax.fori_loop(0, chunks + STEPS + 2, tick, 0)

    def drain(c, _):
        for j in range(1, fast):
            gather_f(j, c).wait_send()
            onward_s(j, c).wait_send()
        for i in range(1, slow):
            gather_s(i, c).wait_send()
            onward_f(i, c).wait_send()
        row_halo(0, c).wait_send()
        row_halo(1, c).wait_send()
        write_out(c).wait()
        for step in range(STEPS):
            @pl.when(has_right)
            def _():
                col_halo(step, 0, c).wait_send()

            @pl.when(has_left)
            def _():
                col_halo(step, 1, c).wait_send()

        return 0

    lax.fori_loop(0, chunks, drain, 0)
    drag_halo(0).wait_send()
    drag_halo(1).wait_send()


def per_device(slow, fast, n_gx, n_gy, ensemble, ancestors, particle_air_drag, eddy_diffusivity):
    levels, rows, cols = ensemble.shape[2:]
    chunks = levels // CHUNK
    block = (PAIR, levels, rows, cols)
    hbm = pl.BlockSpec(memory_space=pltpu.HBM)
    dma = pltpu.SemaphoreType.DMA
    f32 = jnp.float32
    return pl.pallas_call(
        functools.partial(kernel, slow, fast, n_gx, n_gy),
        out_shape=jax.ShapeDtypeStruct(ensemble.shape, f32),
        in_specs=[hbm] * 4,
        out_specs=hbm,
        scratch_shapes=[
            pltpu.VMEM(ensemble.shape, f32),
            pltpu.SMEM(ancestors.shape, jnp.int32),
            pltpu.VMEM((2,) + particle_air_drag.shape[1:], f32),
            pltpu.SMEM(eddy_diffusivity.shape, f32),
            pltpu.VMEM(ensemble.shape, f32),
            *[pltpu.VMEM((2, FIELDS, levels, rows, cols), f32)] * STEPS,
            pltpu.VMEM((STEPS, 2, 2 + FIELDS, rows, cols), f32),
            pltpu.VMEM((fast - 1,) + block, f32),
            pltpu.VMEM((slow - 1,) + block, f32),
            pltpu.VMEM((slow - 1,) + block, f32),
            pltpu.VMEM((fast - 1,) + block, f32),
            pltpu.VMEM((slow - 1,) + block, f32),
            pltpu.VMEM((fast - 1,) + block, f32),
            pltpu.VMEM((STEPS, chunks, rows, cols), f32),
            pltpu.VMEM((STEPS, 2, chunks, rows, cols), f32),
            dma((4,)),
            dma((chunks,)),
            dma((fast - 1, chunks)),
            dma((fast - 1, chunks)),
            dma((slow - 1, chunks)),
            dma((slow - 1, chunks)),
            dma((slow - 1, chunks)),
            dma((slow - 1, chunks)),
            dma((fast - 1, chunks)),
            dma((fast - 1, chunks)),
            dma((2, chunks)),
            dma((2, chunks)),
            dma((STEPS, 2, chunks)),
            dma((STEPS, 2, chunks)),
            dma((2,)),
            dma((2,)),
        ],
        compiler_params=pltpu.CompilerParams(
            collective_id=0, has_side_effects=True, vmem_limit_bytes=32 * 1024 * 1024
        ),
        cost_estimate=pl.CostEstimate(
            flops=STEPS * 60 * math.prod(ensemble.shape),
            bytes_accessed=8 * math.prod(ensemble.shape),
            transcendentals=0,
        ),
    )(ensemble, ancestors, particle_air_drag, eddy_diffusivity)


def solution(mesh):
    members = mesh.shape["dom"]
    fast = max(n for n in range(1, math.isqrt(members) + 1) if members % n == 0)
    placed = (
        P("dom", None, None, "gx", "gy"),
        P(None, "gx", "gy"),
        P("dom", None, "gx", "gy"),
        P(),
    )
    return jax.shard_map(
        functools.partial(
            per_device, members // fast, fast, mesh.shape["gx"], mesh.shape["gy"]
        ),
        mesh=mesh,
        in_specs=placed,
        out_specs=P("dom", None, None, "gx", "gy"),
        check_vma=False,
    )
```

profile of v0, /device:TPU:0, one launch (start us, length us, event | category | flops | bytes accessed | tf_op | source)
XLA Modules:
  0.0 42.8 jit_solution(14548167942492322320)
XLA Ops:
  0.0 0.0 copy-start
  0.0 1.0 %copy-done = f32[1,4,32,8,128]{4,3,2,1,0:T(8,128)S(1)} copy-done((f32[1,4,32,8,128]{4,3,2,1,0:T(8,128)S(1)}, f32[1,4,32,8,128]{4,3,2,1,0:T(8,128)}, u32[]{:S(2)}) %copy-start) | copy-done | bytes 524312
  1.0 0.0 copy-start.1
  1.0 0.7 %copy-done.1 = f32[1,2,8,128]{3,2,1,0:T(8,128)S(1)} copy-done((f32[1,2,8,128]{3,2,1,0:T(8,128)S(1)}, f32[1,2,8,128]{3,2,1,0:T(8,128)}, u32[]{:S(2)}) %copy-start.1) | copy-done | bytes 8216
  1.7 0.0 copy-start.2
  1.7 0.7 %copy-done.2 = s32[4,1,16]{2,1,0:T(1,128)S(1)} copy-done((s32[4,1,16]{2,1,0:T(1,128)S(1)}, s32[4,1,16]{2,1,0:T(1,128)}, u32[]{:S(2)}) %copy-start.2) | copy-done | bytes 280
  2.4 0.0 copy-start.3
  2.4 0.7 %copy-done.3 = f32[31]{0:T(128)S(1)} copy-done((f32[31]{0:T(128)S(1)}, f32[31]{0:T(128)}, u32[]{:S(2)}) %copy-start.3) | copy-done | bytes 148
  3.1 38.9 %shard_map.46 = f32[1,4,32,8,128]{4,3,2,1,0:T(8,128)S(1)} custom-call(f32[1,4,32,8,128]{4,3,2,1,0:T(8,128)S(1)} %copy-done, s32[4,1,16]{2,1,0:T(1,128)S(1)} %copy-done.2, f32[1,2,8,128]{3,2,1,0:T(8,128)S(1)} %copy-done.1, f32[31]{0:T(128)S(1)} %copy-done.3), custom_call_target="tpu_custom_call" | custom-call | flops 31457280 | bytes 1048576 | tf_op jit(solution)/shard_map/pallas_call | solution.py:406
  42.0 0.8 %copy.6 = f32[1,4,32,8,128]{4,3,2,1,0:T(8,128)} copy(f32[1,4,32,8,128]{4,3,2,1,0:T(8,128)S(1)} %shard_map.46) | data formatting | bytes 1048576
Async XLA Ops:
  0.0 1.0 %copy-start = (f32[1,4,32,8,128]{4,3,2,1,0:T(8,128)S(1)}, f32[1,4,32,8,128]{4,3,2,1,0:T(8,128)}, u32[]{:S(2)}) copy-start(f32[1,4,32,8,128]{4,3,2,1,0:T(8,128)} %ens_hbm.1) | copy-start | bytes 1572868
  1.0 0.7 %copy-start.1 = (f32[1,2,8,128]{3,2,1,0:T(8,128)S(1)}, f32[1,2,8,128]{3,2,1,0:T(8,128)}, u32[]{:S(2)}) copy-start(f32[1,2,8,128]{3,2,1,0:T(8,128)} %drag_hbm.1) | copy-start | bytes 24580
  1.7 0.7 %copy-start.2 = (s32[4,1,16]{2,1,0:T(1,128)S(1)}, s32[4,1,16]{2,1,0:T(1,128)}, u32[]{:S(2)}) copy-start(s32[4,1,16]{2,1,0:T(1,128)} %anc_hbm.1) | copy-start | bytes 772
  2.4 0.7 %copy-start.3 = (f32[31]{0:T(128)S(1)}, f32[31]{0:T(128)}, u32[]{:S(2)}) copy-start(f32[31]{0:T(128)} %eddy_hbm.1) | copy-start | bytes 376
where the time goes:
time: 43.2 us; the launch traced here: 42.8 us
  Pallas kernels  38.9 us (90%)
  local copies, waits for them, and re-layouts  3.87 us (9%)
    pallas_call x1, Pallas kernels, per_device(): pl.pallas_call(functools.partial(kernel, slow, fast, n_gx, n_gy), out_sha...  38.9 us
    unnamed x9, local copies, waits for them, and re-layouts  3.87 us

commit v1 on v0

--- a/solution.py
+++ b/solution.py
@@ -11,7 +11,6 @@
 STEPS = 4
 TILE = 8
 CHUNK = 8
-AHEAD = 2
 
 ADVECT = 0.2
 DIFFUSE = 0.15
@@ -40,13 +39,12 @@
 
 def kernel(
     slow, fast, n_gx, n_gy, ens_hbm, anc_hbm, drag_hbm, eddy_hbm, out_hbm,
-    ens, anc, drag, eddy, out, state_0, state_1, state_2, state_3, sums, ag_f, ag_s, tx_f, tx_s, rx_f, rx_s, hy_out, hy_in,
+    ens, anc, drag, eddy, out, state, sums, ag_f, ag_s, tx_f, tx_s, rx_f, rx_s, hy_out, hy_in,
     local_sem, out_sem, agf_send, agf_recv, ags_send, ags_recv, txf_send, txf_recv, txs_send, txs_recv,
     hx_send, hx_recv, hy_send, hy_recv, drag_send, drag_recv,
 ):
     levels, rows, cols = ens.shape[2:]
     chunks = levels // CHUNK
-    states = (state_0, state_1, state_2, state_3)
     me = lax.axis_index("dom")
     a, b = me // fast, me % fast
     gx, gy = lax.axis_index("gx"), lax.axis_index("gy")
@@ -100,11 +98,11 @@
         return pl.ds(c * CHUNK, CHUNK)
 
     def gather_f(j, c):
-        return remote(ens.at[0, 0:PAIR, part(c)], ag_f.at[j - 1, :, part(c)],
+        return remote(ens_hbm.at[0, 0:PAIR, part(c)], ag_f.at[j - 1, :, part(c)],
                       agf_send.at[j - 1, c], agf_recv.at[j - 1, c], at_dom(fast_peer(j)))
 
     def gather_s(i, c):
-        return remote(ens.at[0, PAIR:FIELDS, part(c)], ag_s.at[i - 1, :, part(c)],
+        return remote(ens_hbm.at[0, PAIR:FIELDS, part(c)], ag_s.at[i - 1, :, part(c)],
                       ags_send.at[i - 1, c], ags_recv.at[i - 1, c], at_dom(slow_peer(i)))
 
     def onward_f(i, c):
@@ -118,7 +116,7 @@
     def row_halo(side, c):
         there = at_prev if side == 0 else at_next
         edge = slice(0, STEPS) if side == 0 else slice(rows - STEPS, rows)
-        return remote(state_0.at[0, :, part(c), edge], state_0.at[1, :, part(c), edge],
+        return remote(state.at[0, 0, :, part(c), edge], state.at[0, 1, :, part(c), edge],
                       hx_send.at[side, c], hx_recv.at[side, c], there)
 
     def drag_halo(side):
@@ -159,8 +157,7 @@
         for i in range(1, slow):
             gather_s(i, c).start()
 
-    loads[1].wait()
-    for c in range(min(AHEAD, chunks)):
+    for c in range(chunks):
         start_gather(c)
 
     @pl.when(jnp.logical_not(has_left))
@@ -202,7 +199,7 @@
         for i in range(1, slow):
             hit = hit | (mine == base + i * fast)
         from_s.append(hit)
-    for load in loads[2:]:
+    for load in loads[1:]:
         load.wait()
     drag_halo(0).start()
     drag_halo(1).start()
@@ -230,10 +227,6 @@
                         value = jnp.where(wanted_s[j - 1] == held_s[i - 1], ag_s[i - 1, f, k], value)
                     tx_s[j - 1, f, k] = value
             onward_s(j, c).start()
-
-        @pl.when(c + AHEAD < chunks)
-        def _():
-            start_gather(c + AHEAD)
 
     blank = jnp.zeros((rows, cols), jnp.float32)
 
@@ -265,7 +258,7 @@
                         q = jnp.where(mine == held_s[i - 1], ag_s[i - 1, f - PAIR, k], q)
                     for j in range(1, fast):
                         q = jnp.where(from_s[j - 1], rx_s[j - 1, f - PAIR, k], q)
-                state_0[0, f, k] = q
+                state[0, 0, f, k] = q
         row_halo(0, c).start()
         row_halo(1, c).start()
 
@@ -276,7 +269,7 @@
         for tile in range(2):
             for f in range(FIELDS):
                 for kk in range(CHUNK):
-                    packed = pack(state_0[tile, f, c * CHUNK + kk], place_of(tile, f, kk), packed)
+                    packed = pack(state[0, tile, f, c * CHUNK + kk], place_of(tile, f, kk), packed)
         hy_out[0, c] = packed
         start_columns(0, c)
 
@@ -285,9 +278,7 @@
     half = 0.5 * ADVECT
     temp, salt = 0.5 * PRESS_SCALE * BUOY_TEMP, 0.5 * PRESS_SCALE * BUOY_SALT
 
-    def advance(step, c):
-        final = step == STEPS - 1
-        now_ref, later_ref = states[step], None if final else states[step + 1]
+    def advance(step, c, final):
         tiles = (0,) if final else (0, 1)
         wait_columns(step, c)
         columns = jnp.where(lane % 2 == 0, hy_in[step, 0, c], hy_in[step, 1, c])
@@ -299,7 +290,7 @@
             k = c * CHUNK + kk
             below = jnp.minimum(k + 1, levels - 1)
             mixing = eddy[jnp.minimum(k, levels - 2)]
-            now = [[now_ref[t, f, k] for f in range(FIELDS)] for t in (0, 1)]
+            now = [[state[step, t, f, k] for f in range(FIELDS)] for t in (0, 1)]
             result = [[None] * FIELDS for t in tiles]
             coef = []
             for t in tiles:
@@ -316,7 +307,7 @@
                     edge = pltpu.roll(columns, cols - 1 - place_of(t, f, kk), 1)
                     y_m = pltpu.roll(jnp.where(lane == cols - 1, edge, q), 1, 1)
                     y_p = pltpu.roll(jnp.where(lane == 0, edge, q), cols - 1, 1)
-                    flow = mixing * (now_ref[t, f, below] - q)
+                    flow = mixing * (state[step, t, f, below] - q)
                     total = (1.0 - 4.0 * DIFFUSE) * q + (flow - flux[t][f])
                     c_xm, c_xp, c_ym, c_yp = coef[t]
                     total = total + (c_xp * x_p + c_xm * x_m) + (c_yp * y_p + c_ym * y_m)
@@ -338,7 +329,7 @@
                     if final:
                         out[0, f, k] = result[t][f]
                     else:
-                        later_ref[t, f, k] = result[t][f]
+                        state[step + 1, t, f, k] = result[t][f]
                         packed = pack(result[t][f], place_of(t, f, kk), packed)
         for t in tiles:
             sums[step, t, 0] = press_x[t]
@@ -354,21 +345,33 @@
     drag_halo(0).wait_recv()
     drag_halo(1).wait_recv()
 
+    def every(body):
+        def one(c, _):
+            body(c)
+            return 0
+
+        lax.fori_loop(0, chunks, one, 0)
+
+    every(pass_on)
+    every(resample)
+
     def tick(t, _):
         def at(c, body):
             @pl.when((c >= 0) & (c < chunks))
             def _():
                 body(c)
 
-        at(t, pass_on)
-        at(t - 1, resample)
-        at(t - 2, first_columns)
-
-        for step in range(STEPS):
-            at(t - 3 - step, functools.partial(advance, step))
+        at(t, first_columns)
+
+        def one(step, _):
+            at(t - 1 - step, lambda c: advance(step, c, False))
+            return 0
+
+        lax.fori_loop(0, STEPS - 1, one, 0)
+        at(t - STEPS, lambda c: advance(STEPS - 1, c, True))
         return 0
 
-    lax.fori_loop(0, chunks + STEPS + 2, tick, 0)
+    lax.fori_loop(0, chunks + STEPS, tick, 0)
 
     def drain(c, _):
         for j in range(1, fast):
@@ -414,7 +417,7 @@
             pltpu.VMEM((2,) + particle_air_drag.shape[1:], f32),
             pltpu.SMEM(eddy_diffusivity.shape, f32),
             pltpu.VMEM(ensemble.shape, f32),
-            *[pltpu.VMEM((2, FIELDS, levels, rows, cols), f32)] * STEPS,
+            pltpu.VMEM((STEPS, 2, FIELDS, levels, rows, cols), f32),
             pltpu.VMEM((STEPS, 2, 2 + FIELDS, rows, cols), f32),
             pltpu.VMEM((fast - 1,) + block, f32),
             pltpu.VMEM((slow - 1,) + block, f32),

time: 43.2 us -> 38.8 us (0.90)
  Pallas kernels: 38.9 us -> 34.7 us
    pallas_call x1, Pallas kernels: 38.9 us -> 34.7 us  [per_device(): pl.pallas_call(functools.partial(kernel, slow, fast, n_gx, n_gy), out_sha...]
where the time goes in v1:
time: 38.8 us; the launch traced here: 38.6 us
  Pallas kernels  34.7 us (89%)
  local copies, waits for them, and re-layouts  3.87 us (10%)
    pallas_call x1, Pallas kernels, per_device(): pl.pallas_call(functools.partial(kernel, slow, fast, n_gx, n_gy), out_sha...  34.7 us
    unnamed x9, local copies, waits for them, and re-layouts  3.87 us

profile of v1, /device:TPU:0, one launch (start us, length us, event | category | flops | bytes accessed | tf_op | source)
XLA Modules:
  0.0 38.6 jit_solution(13601911014293149076)
XLA Ops:
  0.0 0.0 copy-start
  0.0 1.0 %copy-done = f32[1,4,32,8,128]{4,3,2,1,0:T(8,128)S(1)} copy-done((f32[1,4,32,8,128]{4,3,2,1,0:T(8,128)S(1)}, f32[1,4,32,8,128]{4,3,2,1,0:T(8,128)}, u32[]{:S(2)}) %copy-start) | copy-done | bytes 524312
  1.0 0.0 copy-start.1
  1.0 0.7 %copy-done.1 = f32[1,2,8,128]{3,2,1,0:T(8,128)S(1)} copy-done((f32[1,2,8,128]{3,2,1,0:T(8,128)S(1)}, f32[1,2,8,128]{3,2,1,0:T(8,128)}, u32[]{:S(2)}) %copy-start.1) | copy-done | bytes 8216
  1.7 0.0 copy-start.2
  1.7 0.7 %copy-done.2 = s32[4,1,16]{2,1,0:T(1,128)S(1)} copy-done((s32[4,1,16]{2,1,0:T(1,128)S(1)}, s32[4,1,16]{2,1,0:T(1,128)}, u32[]{:S(2)}) %copy-start.2) | copy-done | bytes 280
  2.4 0.0 copy-start.3
  2.4 0.7 %copy-done.3 = f32[31]{0:T(128)S(1)} copy-done((f32[31]{0:T(128)S(1)}, f32[31]{0:T(128)}, u32[]{:S(2)}) %copy-start.3) | copy-done | bytes 148
  3.1 34.7 %shard_map.46 = f32[1,4,32,8,128]{4,3,2,1,0:T(8,128)S(1)} custom-call(f32[1,4,32,8,128]{4,3,2,1,0:T(8,128)S(1)} %copy-done, s32[4,1,16]{2,1,0:T(1,128)S(1)} %copy-done.2, f32[1,2,8,128]{3,2,1,0:T(8,128)S(1)} %copy-done.1, f32[31]{0:T(128)S(1)} %copy-done.3), custom_call_target="tpu_custom_call" | custom-call | flops 31457280 | bytes 1048576 | tf_op jit(solution)/shard_map/pallas_call | solution.py:409
  37.8 0.8 %copy.6 = f32[1,4,32,8,128]{4,3,2,1,0:T(8,128)} copy(f32[1,4,32,8,128]{4,3,2,1,0:T(8,128)S(1)} %shard_map.46) | data formatting | bytes 1048576
Async XLA Ops:
  0.0 1.0 %copy-start = (f32[1,4,32,8,128]{4,3,2,1,0:T(8,128)S(1)}, f32[1,4,32,8,128]{4,3,2,1,0:T(8,128)}, u32[]{:S(2)}) copy-start(f32[1,4,32,8,128]{4,3,2,1,0:T(8,128)} %ens_hbm.1) | copy-start | bytes 1572868
  1.0 0.7 %copy-start.1 = (f32[1,2,8,128]{3,2,1,0:T(8,128)S(1)}, f32[1,2,8,128]{3,2,1,0:T(8,128)}, u32[]{:S(2)}) copy-start(f32[1,2,8,128]{3,2,1,0:T(8,128)} %drag_hbm.1) | copy-start | bytes 24580
  1.7 0.7 %copy-start.2 = (s32[4,1,16]{2,1,0:T(1,128)S(1)}, s32[4,1,16]{2,1,0:T(1,128)}, u32[]{:S(2)}) copy-start(s32[4,1,16]{2,1,0:T(1,128)} %anc_hbm.1) | copy-start | bytes 772
  2.4 0.7 %copy-start.3 = (f32[31]{0:T(128)S(1)}, f32[31]{0:T(128)}, u32[]{:S(2)}) copy-start(f32[31]{0:T(128)} %eddy_hbm.1) | copy-start | bytes 376

commit v2 on v1

--- a/solution.py
+++ b/solution.py
@@ -10,7 +10,7 @@
 
 STEPS = 4
 TILE = 8
-CHUNK = 8
+CHUNK = 4
 
 ADVECT = 0.2
 DIFFUSE = 0.15

time: 38.8 us -> 39.3 us (1.013)
  Pallas kernels: 34.7 us -> 35.2 us
    pallas_call x1, Pallas kernels: 34.7 us -> 35.2 us  [per_device(): pl.pallas_call(functools.partial(kernel, slow, fast, n_gx, n_gy), out_sha...]
where the time goes in v2:
time: 39.3 us; the launch traced here: 39 us
  Pallas kernels  35.2 us (90%)
  local copies, waits for them, and re-layouts  3.87 us (10%)
    pallas_call x1, Pallas kernels, per_device(): pl.pallas_call(functools.partial(kernel, slow, fast, n_gx, n_gy), out_sha...  35.2 us
    unnamed x9, local copies, waits for them, and re-layouts  3.87 us

profile of v2, /device:TPU:0, one launch (start us, length us, event | category | flops | bytes accessed | tf_op | source)
XLA Modules:
  0.0 39.0 jit_solution(17208590404548643284)
XLA Ops:
  0.0 0.0 copy-start
  0.0 1.0 %copy-done = f32[1,4,32,8,128]{4,3,2,1,0:T(8,128)S(1)} copy-done((f32[1,4,32,8,128]{4,3,2,1,0:T(8,128)S(1)}, f32[1,4,32,8,128]{4,3,2,1,0:T(8,128)}, u32[]{:S(2)}) %copy-start) | copy-done | bytes 524312
  1.0 0.0 copy-start.1
  1.0 0.7 %copy-done.1 = f32[1,2,8,128]{3,2,1,0:T(8,128)S(1)} copy-done((f32[1,2,8,128]{3,2,1,0:T(8,128)S(1)}, f32[1,2,8,128]{3,2,1,0:T(8,128)}, u32[]{:S(2)}) %copy-start.1) | copy-done | bytes 8216
  1.7 0.0 copy-start.2
  1.7 0.7 %copy-done.2 = s32[4,1,16]{2,1,0:T(1,128)S(1)} copy-done((s32[4,1,16]{2,1,0:T(1,128)S(1)}, s32[4,1,16]{2,1,0:T(1,128)}, u32[]{:S(2)}) %copy-start.2) | copy-done | bytes 280
  2.4 0.0 copy-start.3
  2.4 0.7 %copy-done.3 = f32[31]{0:T(128)S(1)} copy-done((f32[31]{0:T(128)S(1)}, f32[31]{0:T(128)}, u32[]{:S(2)}) %copy-start.3) | copy-done | bytes 148
  3.1 35.2 %shard_map.46 = f32[1,4,32,8,128]{4,3,2,1,0:T(8,128)S(1)} custom-call(f32[1,4,32,8,128]{4,3,2,1,0:T(8,128)S(1)} %copy-done, s32[4,1,16]{2,1,0:T(1,128)S(1)} %copy-done.2, f32[1,2,8,128]{3,2,1,0:T(8,128)S(1)} %copy-done.1, f32[31]{0:T(128)S(1)} %copy-done.3), custom_call_target="tpu_custom_call" | custom-call | flops 31457280 | bytes 1048576 | tf_op jit(solution)/shard_map/pallas_call | solution.py:409
  38.2 0.8 %copy.6 = f32[1,4,32,8,128]{4,3,2,1,0:T(8,128)} copy(f32[1,4,32,8,128]{4,3,2,1,0:T(8,128)S(1)} %shard_map.46) | data formatting | bytes 1048576
Async XLA Ops:
  0.0 1.0 %copy-start = (f32[1,4,32,8,128]{4,3,2,1,0:T(8,128)S(1)}, f32[1,4,32,8,128]{4,3,2,1,0:T(8,128)}, u32[]{:S(2)}) copy-start(f32[1,4,32,8,128]{4,3,2,1,0:T(8,128)} %ens_hbm.1) | copy-start | bytes 1572868
  1.0 0.7 %copy-start.1 = (f32[1,2,8,128]{3,2,1,0:T(8,128)S(1)}, f32[1,2,8,128]{3,2,1,0:T(8,128)}, u32[]{:S(2)}) copy-start(f32[1,2,8,128]{3,2,1,0:T(8,128)} %drag_hbm.1) | copy-start | bytes 24580
  1.7 0.7 %copy-start.2 = (s32[4,1,16]{2,1,0:T(1,128)S(1)}, s32[4,1,16]{2,1,0:T(1,128)}, u32[]{:S(2)}) copy-start(s32[4,1,16]{2,1,0:T(1,128)} %anc_hbm.1) | copy-start | bytes 772
  2.4 0.7 %copy-start.3 = (f32[31]{0:T(128)S(1)}, f32[31]{0:T(128)}, u32[]{:S(2)}) copy-start(f32[31]{0:T(128)} %eddy_hbm.1) | copy-start | bytes 376

commit v3 on v1

--- a/solution.py
+++ b/solution.py
@@ -11,6 +11,7 @@
 STEPS = 4
 TILE = 8
 CHUNK = 8
+AHEAD = 2
 
 ADVECT = 0.2
 DIFFUSE = 0.15
@@ -157,7 +158,7 @@
         for i in range(1, slow):
             gather_s(i, c).start()
 
-    for c in range(chunks):
+    for c in range(min(AHEAD, chunks)):
         start_gather(c)
 
     @pl.when(jnp.logical_not(has_left))
@@ -227,6 +228,10 @@
                         value = jnp.where(wanted_s[j - 1] == held_s[i - 1], ag_s[i - 1, f, k], value)
                     tx_s[j - 1, f, k] = value
             onward_s(j, c).start()
+
+        @pl.when(c + AHEAD < chunks)
+        def _():
+            start_gather(c + AHEAD)
 
     blank = jnp.zeros((rows, cols), jnp.float32)
 
@@ -345,22 +350,19 @@
     drag_halo(0).wait_recv()
     drag_halo(1).wait_recv()
 
-    def every(body):
-        def one(c, _):
+    def at(c, body):
+        @pl.when((c >= 0) & (c < chunks))
+        def _():
             body(c)
-            return 0
-
-        lax.fori_loop(0, chunks, one, 0)
-
-    every(pass_on)
-    every(resample)
+
+    def exchange(t, _):
+        at(t, pass_on)
+        at(t - 2, resample)
+        return 0
+
+    lax.fori_loop(0, chunks + 2, exchange, 0)
 
     def tick(t, _):
-        def at(c, body):
-            @pl.when((c >= 0) & (c < chunks))
-            def _():
-                body(c)
-
         at(t, first_columns)
 
         def one(step, _):

time: 38.8 us -> 38.3 us (0.987)
  Pallas kernels: 34.7 us -> 34.2 us
    pallas_call x1, Pallas kernels: 34.7 us -> 34.2 us  [per_device(): pl.pallas_call(functools.partial(kernel, slow, fast, n_gx, n_gy), out_sha...]
where the time goes in v3:
time: 38.3 us; the launch traced here: 38 us
  Pallas kernels  34.2 us (89%)
  local copies, waits for them, and re-layouts  3.87 us (10%)
    pallas_call x1, Pallas kernels, per_device(): pl.pallas_call(functools.partial(kernel, slow, fast, n_gx, n_gy), out_sha...  34.2 us
    unnamed x9, local copies, waits for them, and re-layouts  3.87 us

profile of v3, /device:TPU:0, one launch (start us, length us, event | category | flops | bytes accessed | tf_op | source)
XLA Modules:
  0.0 38.0 jit_solution(12850286239243605508)
XLA Ops:
  0.0 0.0 copy-start
  0.0 1.0 %copy-done = f32[1,4,32,8,128]{4,3,2,1,0:T(8,128)S(1)} copy-done((f32[1,4,32,8,128]{4,3,2,1,0:T(8,128)S(1)}, f32[1,4,32,8,128]{4,3,2,1,0:T(8,128)}, u32[]{:S(2)}) %copy-start) | copy-done | bytes 524312
  1.0 0.0 copy-start.1
  1.0 0.7 %copy-done.1 = f32[1,2,8,128]{3,2,1,0:T(8,128)S(1)} copy-done((f32[1,2,8,128]{3,2,1,0:T(8,128)S(1)}, f32[1,2,8,128]{3,2,1,0:T(8,128)}, u32[]{:S(2)}) %copy-start.1) | copy-done | bytes 8216
  1.7 0.0 copy-start.2
  1.7 0.7 %copy-done.2 = s32[4,1,16]{2,1,0:T(1,128)S(1)} copy-done((s32[4,1,16]{2,1,0:T(1,128)S(1)}, s32[4,1,16]{2,1,0:T(1,128)}, u32[]{:S(2)}) %copy-start.2) | copy-done | bytes 280
  2.4 0.0 copy-start.3
  2.4 0.7 %copy-done.3 = f32[31]{0:T(128)S(1)} copy-done((f32[31]{0:T(128)S(1)}, f32[31]{0:T(128)}, u32[]{:S(2)}) %copy-start.3) | copy-done | bytes 148
  3.1 34.2 %shard_map.46 = f32[1,4,32,8,128]{4,3,2,1,0:T(8,128)S(1)} custom-call(f32[1,4,32,8,128]{4,3,2,1,0:T(8,128)S(1)} %copy-done, s32[4,1,16]{2,1,0:T(1,128)S(1)} %copy-done.2, f32[1,2,8,128]{3,2,1,0:T(8,128)S(1)} %copy-done.1, f32[31]{0:T(128)S(1)} %copy-done.3), custom_call_target="tpu_custom_call" | custom-call | flops 31457280 | bytes 1048576 | tf_op jit(solution)/shard_map/pallas_call | solution.py:411
  37.2 0.8 %copy.6 = f32[1,4,32,8,128]{4,3,2,1,0:T(8,128)} copy(f32[1,4,32,8,128]{4,3,2,1,0:T(8,128)S(1)} %shard_map.46) | data formatting | bytes 1048576
Async XLA Ops:
  0.0 1.0 %copy-start = (f32[1,4,32,8,128]{4,3,2,1,0:T(8,128)S(1)}, f32[1,4,32,8,128]{4,3,2,1,0:T(8,128)}, u32[]{:S(2)}) copy-start(f32[1,4,32,8,128]{4,3,2,1,0:T(8,128)} %ens_hbm.1) | copy-start | bytes 1572868
  1.0 0.7 %copy-start.1 = (f32[1,2,8,128]{3,2,1,0:T(8,128)S(1)}, f32[1,2,8,128]{3,2,1,0:T(8,128)}, u32[]{:S(2)}) copy-start(f32[1,2,8,128]{3,2,1,0:T(8,128)} %drag_hbm.1) | copy-start | bytes 24580
  1.7 0.7 %copy-start.2 = (s32[4,1,16]{2,1,0:T(1,128)S(1)}, s32[4,1,16]{2,1,0:T(1,128)}, u32[]{:S(2)}) copy-start(s32[4,1,16]{2,1,0:T(1,128)} %anc_hbm.1) | copy-start | bytes 772
  2.4 0.7 %copy-start.3 = (f32[31]{0:T(128)S(1)}, f32[31]{0:T(128)}, u32[]{:S(2)}) copy-start(f32[31]{0:T(128)} %eddy_hbm.1) | copy-start | bytes 376

commit v4 on v3

--- a/solution.py
+++ b/solution.py
@@ -39,9 +39,9 @@
 
 
 def kernel(
-    slow, fast, n_gx, n_gy, ens_hbm, anc_hbm, drag_hbm, eddy_hbm, out_hbm,
-    ens, anc, drag, eddy, out, state, sums, ag_f, ag_s, tx_f, tx_s, rx_f, rx_s, hy_out, hy_in,
-    local_sem, out_sem, agf_send, agf_recv, ags_send, ags_recv, txf_send, txf_recv, txs_send, txs_recv,
+    slow, fast, n_gx, n_gy, ens_hbm, anc_hbm, drag_hbm, eddy_hbm, out,
+    ens, anc, drag, eddy, state, sums, ag_f, ag_s, tx_f, tx_s, rx_f, rx_s, hy_out, hy_in,
+    local_sem, agf_send, agf_recv, ags_send, ags_recv, txf_send, txf_recv, txs_send, txs_recv,
     hx_send, hx_recv, hy_send, hy_recv, drag_send, drag_recv,
 ):
     levels, rows, cols = ens.shape[2:]
@@ -130,9 +130,6 @@
         there = at_right if side == 0 else at_left
         return remote(hy_out.at[step, c], hy_in.at[step, side, c],
                       hy_send.at[step, side, c], hy_recv.at[step, side, c], there)
-
-    def write_out(c):
-        return pltpu.make_async_copy(out.at[:, :, part(c)], out_hbm.at[:, :, part(c)], out_sem.at[c])
 
     def start_columns(step, c):
         @pl.when(has_right)
@@ -341,9 +338,7 @@
             sums[step, t, 1] = press_y[t]
             for f in range(FIELDS):
                 sums[step, t, 2 + f] = flux[t][f]
-        if final:
-            write_out(c).start()
-        else:
+        if not final:
             hy_out[step + 1, c] = packed
             start_columns(step + 1, c)
 
@@ -384,7 +379,6 @@
             onward_f(i, c).wait_send()
         row_halo(0, c).wait_send()
         row_halo(1, c).wait_send()
-        write_out(c).wait()
         for step in range(STEPS):
             @pl.when(has_right)
             def _():
@@ -412,13 +406,12 @@
         functools.partial(kernel, slow, fast, n_gx, n_gy),
         out_shape=jax.ShapeDtypeStruct(ensemble.shape, f32),
         in_specs=[hbm] * 4,
-        out_specs=hbm,
+        out_specs=pl.BlockSpec(memory_space=pltpu.VMEM),
         scratch_shapes=[
             pltpu.VMEM(ensemble.shape, f32),
             pltpu.SMEM(ancestors.shape, jnp.int32),
             pltpu.VMEM((2,) + particle_air_drag.shape[1:], f32),
             pltpu.SMEM(eddy_diffusivity.shape, f32),
-            pltpu.VMEM(ensemble.shape, f32),
             pltpu.VMEM((STEPS, 2, FIELDS, levels, rows, cols), f32),
             pltpu.VMEM((STEPS, 2, 2 + FIELDS, rows, cols), f32),
             pltpu.VMEM((fast - 1,) + block, f32),
@@ -430,7 +423,6 @@
             pltpu.VMEM((STEPS, chunks, rows, cols), f32),
             pltpu.VMEM((STEPS, 2, chunks, rows, cols), f32),
             dma((4,)),
-            dma((chunks,)),
             dma((fast - 1, chunks)),
             dma((fast - 1, chunks)),
             dma((slow - 1, chunks)),

time: 38.3 us -> 38.1 us (level)
  no operation moved by 1% of the time
where the time goes in v4:
time: 38.1 us; the launch traced here: 37.9 us
  Pallas kernels  34 us (89%)
  local copies, waits for them, and re-layouts  3.87 us (10%)
    pallas_call x1, Pallas kernels, per_device(): pl.pallas_call(functools.partial(kernel, slow, fast, n_gx, n_gy), out_sha...  34 us
    unnamed x9, local copies, waits for them, and re-layouts  3.87 us

profile of v4, /device:TPU:0, one launch (start us, length us, event | category | flops | bytes accessed | tf_op | source)
XLA Modules:
  0.0 37.9 jit_solution(8241327425793455456)
XLA Ops:
  0.0 0.0 copy-start
  0.0 1.0 %copy-done = f32[1,4,32,8,128]{4,3,2,1,0:T(8,128)S(1)} copy-done((f32[1,4,32,8,128]{4,3,2,1,0:T(8,128)S(1)}, f32[1,4,32,8,128]{4,3,2,1,0:T(8,128)}, u32[]{:S(2)}) %copy-start) | copy-done | bytes 524312
  1.0 0.0 copy-start.1
  1.0 0.7 %copy-done.1 = f32[1,2,8,128]{3,2,1,0:T(8,128)S(1)} copy-done((f32[1,2,8,128]{3,2,1,0:T(8,128)S(1)}, f32[1,2,8,128]{3,2,1,0:T(8,128)}, u32[]{:S(2)}) %copy-start.1) | copy-done | bytes 8216
  1.7 0.0 copy-start.2
  1.7 0.7 %copy-done.2 = s32[4,1,16]{2,1,0:T(1,128)S(1)} copy-done((s32[4,1,16]{2,1,0:T(1,128)S(1)}, s32[4,1,16]{2,1,0:T(1,128)}, u32[]{:S(2)}) %copy-start.2) | copy-done | bytes 280
  2.4 0.0 copy-start.3
  2.4 0.7 %copy-done.3 = f32[31]{0:T(128)S(1)} copy-done((f32[31]{0:T(128)S(1)}, f32[31]{0:T(128)}, u32[]{:S(2)}) %copy-start.3) | copy-done | bytes 148
  3.1 34.0 %shard_map.46 = f32[1,4,32,8,128]{4,3,2,1,0:T(8,128)S(1)} custom-call(f32[1,4,32,8,128]{4,3,2,1,0:T(8,128)S(1)} %copy-done, s32[4,1,16]{2,1,0:T(1,128)S(1)} %copy-done.2, f32[1,2,8,128]{3,2,1,0:T(8,128)S(1)} %copy-done.1, f32[31]{0:T(128)S(1)} %copy-done.3), custom_call_target="tpu_custom_call" | custom-call | flops 31457280 | bytes 1048576 | tf_op jit(solution)/shard_map/pallas_call | solution.py:405
  37.1 0.8 %copy.6 = f32[1,4,32,8,128]{4,3,2,1,0:T(8,128)} copy(f32[1,4,32,8,128]{4,3,2,1,0:T(8,128)S(1)} %shard_map.46) | data formatting | bytes 1048576
Async XLA Ops:
  0.0 1.0 %copy-start = (f32[1,4,32,8,128]{4,3,2,1,0:T(8,128)S(1)}, f32[1,4,32,8,128]{4,3,2,1,0:T(8,128)}, u32[]{:S(2)}) copy-start(f32[1,4,32,8,128]{4,3,2,1,0:T(8,128)} %ens_hbm.1) | copy-start | bytes 1572868
  1.0 0.7 %copy-start.1 = (f32[1,2,8,128]{3,2,1,0:T(8,128)S(1)}, f32[1,2,8,128]{3,2,1,0:T(8,128)}, u32[]{:S(2)}) copy-start(f32[1,2,8,128]{3,2,1,0:T(8,128)} %drag_hbm.1) | copy-start | bytes 24580
  1.7 0.7 %copy-start.2 = (s32[4,1,16]{2,1,0:T(1,128)S(1)}, s32[4,1,16]{2,1,0:T(1,128)}, u32[]{:S(2)}) copy-start(s32[4,1,16]{2,1,0:T(1,128)} %anc_hbm.1) | copy-start | bytes 772
  2.4 0.7 %copy-start.3 = (f32[31]{0:T(128)S(1)}, f32[31]{0:T(128)}, u32[]{:S(2)}) copy-start(f32[31]{0:T(128)} %eddy_hbm.1) | copy-start | bytes 376
